TPU v7x, 128 devices: a whole 4x4x4 slice. The times are simulated.
128 devices in a mesh: row: 8 (over x, core), col: 16 (over y, z).
Axes of the slice: x: 4, y: 4, z: 4, core: 2. Of those that a mesh axis runs over, the one named last changes fastest.
Arguments:
- object_slices: float32 [2, 2, 2048, 4096], P(None, None, 'row', 'col'), may hold values from -5 to 5
- probe: float32 [2, 128, 128], replicated, may hold values from -6 to 6
- amplitudes: float32 [8, 16, 16, 128, 128], P('row', 'col'), may hold values from 0.3 to 3
- scan_pos: int32 [2, 8, 16, 16], P(None, 'row', 'col'), may hold values from 0 to 4095, as said below
- scan_count: int32 [8, 16], P('row', 'col'), may hold values from 0 to 16, as said below
Outputs:
- object_new: float32 [2, 2, 2048, 4096], P(None, None, 'row', 'col')
Inputs may be any that keep to these rules, and one draw needn't show every extreme that they name: `scan_pos`: entry [0, i, j, k] is the pixel row and [1, i, j, k] the pixel column of the centre of slot k of tile (i, j); the centre lies within that tile's 256 x 256 pixels, also for slots that are not live. The live scans of a tile are its first scan_count slots; in every tile row the counts of its 16 tiles sum to exactly 128, and some tile of every row holds 16 scans.
All inputs are finite; a program needn't handle non-finite values.
Results may differ from a plain program's by a relative error of at most 0.00029.
Values sent between devices are 32-bit elements; how exact they have to be, the bound alone decides.
A program may use at most 128 MiB of HBM per device.

v0:
```python
import math

import jax
import jax.numpy as jnp
from jax import lax
from jax.sharding import PartitionSpec as P

ITERS = 2


modulus_offset = 0.5
fresnel_scale = 0.9
highest = lax.Precision.HIGHEST


def entering(value, axis, join, neutral):
    count, mine = (lax.axis_size(axis), lax.axis_index(axis))
    pieces = lax.all_gather(value, axis)
    running = jnp.full_like(value, 0) + jnp.asarray(neutral, value.dtype)

    def hop(position, running):
        longer = join(running, pieces[position])
        return jnp.where(position < mine, longer, running)

    return lax.fori_loop(0, count - 1, hop, running)


def with_halo(cells, sides, width):
    for axis, dim in sides:
        count = lax.axis_size(axis)
        ends = count - 1
        head = lax.slice_in_dim(cells, 0, width, axis=dim)
        tail = lax.slice_in_dim(cells, cells.shape[dim] - width, cells.shape[dim], axis=dim)
        cells = jnp.concatenate(
            [
                lax.ppermute(tail, axis, [(i, (i + 1) % count) for i in range(ends)]),
                cells,
                lax.ppermute(head, axis, [((i + 1) % count, i) for i in range(ends)]),
            ],
            axis=dim,
        )
    return cells


def dft_tables(frame_size):
    positions = jnp.arange(frame_size, dtype=jnp.int32)
    wrapped = positions[:, None] * positions[None, :] % frame_size
    angles = -2.0 * math.pi / frame_size * wrapped.astype(jnp.float32)
    scaling = 1.0 / math.sqrt(frame_size)
    return (jnp.cos(angles) * scaling, jnp.sin(angles) * scaling)


def propagator(frame_size):
    positions = jnp.arange(frame_size, dtype=jnp.int32)
    frequency = jnp.where(positions < frame_size // 2, positions, positions - frame_size).astype(
        jnp.float32
    )
    phase = (
        math.pi * fresnel_scale * (frequency[:, None] ** 2 + frequency[None, :] ** 2) / frame_size
    )
    return (jnp.cos(phase), jnp.sin(phase))


def apply_left(matrix, values):
    return jnp.einsum("jk,bkl->bjl", matrix, values, precision=highest)


def apply_right(values, matrix):
    return jnp.einsum("bjk,kl->bjl", values, matrix, precision=highest)


def transform(real_part, imag_part, table_re, table_im):
    mid_re = apply_left(table_re, real_part) - apply_left(table_im, imag_part)
    mid_im = apply_left(table_re, imag_part) + apply_left(table_im, real_part)
    out_re = apply_right(mid_re, table_re) - apply_right(mid_im, table_im)
    out_im = apply_right(mid_re, table_im) + apply_right(mid_im, table_re)
    return (out_re, out_im)


def slot_gradients(patches, local_amps, weights, probe, tables):
    table_re, table_im, inverse_im, prop_re, prop_im = tables
    layers = patches.shape[1]
    obj_re = [patches[:, layer_id, 0] for layer_id in range(layers)]
    obj_im = [patches[:, layer_id, 1] for layer_id in range(layers)]
    inc_re = [jnp.broadcast_to(probe[0], local_amps.shape)]
    inc_im = [jnp.broadcast_to(probe[1], local_amps.shape)]
    layer_id = 0
    exit_re = inc_re[layer_id] * obj_re[layer_id] - inc_im[layer_id] * obj_im[layer_id]
    exit_im = inc_re[layer_id] * obj_im[layer_id] + inc_im[layer_id] * obj_re[layer_id]
    spec_re, spec_im = transform(exit_re, exit_im, table_re, table_im)
    spec_re, spec_im = (
        spec_re * prop_re - spec_im * prop_im,
        spec_re * prop_im + spec_im * prop_re,
    )
    next_re, next_im = transform(spec_re, spec_im, table_re, inverse_im)
    inc_re.append(next_re)
    inc_im.append(next_im)
    exit_re = inc_re[-1] * obj_re[-1] - inc_im[-1] * obj_im[-1]
    exit_im = inc_re[-1] * obj_im[-1] + inc_im[-1] * obj_re[-1]
    psi_re, psi_im = transform(exit_re, exit_im, table_re, table_im)
    modulus = jnp.sqrt(psi_re * psi_re + psi_im * psi_im + modulus_offset)
    factor = 1.0 - local_amps / modulus
    back_re, back_im = transform(psi_re * factor, psi_im * factor, table_re, inverse_im)
    gradients = [None] * layers
    for layer_id in reversed(range(layers)):
        grad_re = inc_re[layer_id] * back_re + inc_im[layer_id] * back_im
        grad_im = inc_re[layer_id] * back_im - inc_im[layer_id] * back_re
        gradients[layer_id] = jnp.stack([grad_re, grad_im], axis=1)
        if layer_id > 0:
            adj_re = obj_re[layer_id] * back_re + obj_im[layer_id] * back_im
            adj_im = obj_re[layer_id] * back_im - obj_im[layer_id] * back_re
            spec_re, spec_im = transform(adj_re, adj_im, table_re, table_im)
            spec_re, spec_im = (
                spec_re * prop_re + spec_im * prop_im,
                spec_im * prop_re - spec_re * prop_im,
            )
            back_re, back_im = transform(spec_re, spec_im, table_re, inverse_im)
    return jnp.stack(gradients, axis=1) * weights[:, None, None, None, None]


def cut_patches(extended, patch_row, patch_col, frame_size):
    layers = extended.shape[0]
    zero_index = jnp.zeros((), jnp.int32)
    return jax.vmap(
        lambda row_at, col_at: lax.dynamic_slice(
            extended, (zero_index, zero_index, row_at, col_at), (layers, 2, frame_size, frame_size)
        )
    )(patch_row, patch_col)


def place_patches(ext_shape, gradients, patch_row, patch_col):
    zero_index = jnp.zeros((), jnp.int32)

    def add_one(item, accumulator):
        corner = (zero_index, zero_index, patch_row[item], patch_col[item])
        current_block = lax.dynamic_slice(accumulator, corner, gradients.shape[1:])
        return lax.dynamic_update_slice(accumulator, current_block + gradients[item], corner)

    return lax.fori_loop(0, gradients.shape[0], add_one, jnp.zeros(ext_shape, jnp.float32))


def fold_axis(widened, rim_width, frame_size, along_axis):
    total_len = widened.shape[along_axis] - 2 * rim_width
    inner_len = total_len - frame_size
    middle = lax.slice_in_dim(widened, rim_width, rim_width + total_len, axis=along_axis)
    lower_rim = lax.slice_in_dim(widened, 0, rim_width, axis=along_axis)
    upper_rim = lax.slice_in_dim(
        widened, rim_width + total_len, total_len + 2 * rim_width, axis=along_axis
    )
    lower_place = [slice(None)] * widened.ndim
    lower_place[along_axis] = slice(frame_size - rim_width, frame_size)
    upper_place = [slice(None)] * widened.ndim
    upper_place[along_axis] = slice(inner_len, inner_len + rim_width)
    return middle.at[tuple(lower_place)].add(lower_rim).at[tuple(upper_place)].add(upper_rim)


def fold_rims(widened, rim_width, frame_size):
    return fold_axis(fold_axis(widened, rim_width, frame_size, 2), rim_width, frame_size, 3)


def add_counts(earlier, later):
    return earlier + later


def body(object_slices, probe, amplitudes, scan_pos, scan_count):
    layers, _, tile_r, tile_c = object_slices.shape
    frame_size = probe.shape[-1]
    half_frame = frame_size // 2
    own_slots = amplitudes.shape[2]
    work_slots = own_slots // 2
    col_count = lax.axis_size("col")
    row_start = lax.axis_index("row") * tile_r
    col_start = lax.axis_index("col") * tile_c
    patch_row = scan_pos[0, 0, 0] - row_start
    patch_col = scan_pos[1, 0, 0] - col_start
    local_amps = amplitudes[0, 0]
    tile_count = scan_count[0, 0]
    slot_ids = jnp.arange(own_slots, dtype=jnp.int32)
    live_mask = (slot_ids < tile_count).astype(jnp.float32)
    table_re, table_im = dft_tables(frame_size)
    prop_re, prop_im = propagator(frame_size)
    tables = (table_re, table_im, -table_im, prop_re, prop_im)
    ext_shape = (layers, 2, tile_r + frame_size, tile_c + frame_size)
    prefix = entering(jnp.reshape(tile_count, (1,)), "col", add_counts, jnp.zeros((1,), jnp.int32))[
        0
    ]
    per_peer = own_slots // col_count
    rotation = prefix % col_count
    position = (rotation + slot_ids) % col_count * per_peer + slot_ids // col_count
    send_order = slot_ids % per_peer * col_count + (slot_ids // per_peer - rotation) % col_count
    outgoing_live = jnp.take(live_mask, send_order).reshape(col_count, per_peer)
    outgoing_amps = jnp.take(local_amps, send_order, axis=0).reshape(
        col_count, per_peer, frame_size, frame_size
    )
    worker_state = None
    current = object_slices
    for iteration in range(ITERS):
        extended = with_halo(current, (("row", 2), ("col", 3)), half_frame)
        gradient_worker_state = worker_state
        patches = cut_patches(extended, patch_row, patch_col, frame_size)
        outgoing = jnp.take(patches, send_order, axis=0).reshape(
            col_count, per_peer, layers, 2, frame_size, frame_size
        )
        if gradient_worker_state is None:
            got_patches, got_amps, got_live = (
                lax.all_to_all(outgoing, "col", split_axis=0, concat_axis=0, tiled=True),
                lax.all_to_all(outgoing_amps, "col", split_axis=0, concat_axis=0, tiled=True),
                lax.all_to_all(outgoing_live, "col", split_axis=0, concat_axis=0, tiled=True),
            )
            flag_values = got_live.reshape(own_slots)
            flag_ints = flag_values.astype(jnp.int32)
            slot_rank = jnp.cumsum(flag_ints) - 1
            chosen = (slot_rank[:, None] == jnp.arange(work_slots, dtype=jnp.int32)[None, :]) & (
                flag_ints[:, None] == 1
            )
            picked = jnp.sum(jnp.where(chosen, slot_ids[:, None], 0), axis=0)
            work_amps = jnp.take(
                got_amps.reshape(own_slots, frame_size, frame_size), picked, axis=0
            )
            gradient_worker_state = (flag_values, slot_rank, picked, work_amps)
        else:
            got_patches = lax.all_to_all(outgoing, "col", split_axis=0, concat_axis=0, tiled=True)
        flag_values, slot_rank, picked, work_amps = gradient_worker_state
        work_patches = jnp.take(
            got_patches.reshape(own_slots, layers, 2, frame_size, frame_size), picked, axis=0
        )
        work_grads = slot_gradients(
            work_patches, work_amps, jnp.ones((work_slots,), jnp.float32), probe, tables
        )
        returned = (
            jnp.take(work_grads, jnp.clip(slot_rank, 0, work_slots - 1), axis=0)
            * flag_values[:, None, None, None, None]
        )
        returned_grads = lax.all_to_all(
            returned.reshape(col_count, per_peer, layers, 2, frame_size, frame_size),
            "col",
            split_axis=0,
            concat_axis=0,
            tiled=True,
        )
        gradients = jnp.take(
            returned_grads.reshape(own_slots, layers, 2, frame_size, frame_size), position, axis=0
        )
        grad_ext = place_patches(ext_shape, gradients, patch_row, patch_col)
        worker_state = gradient_worker_state
        widened = with_halo(grad_ext, (("row", 2), ("col", 3)), half_frame)
        summed = fold_rims(widened, half_frame, frame_size)
        current = (
            current
            - summed[:, :, half_frame : half_frame + tile_r, half_frame : half_frame + tile_c]
        )
    return current


def solution(mesh):
    in_specs = (
        P(None, None, "row", "col"),
        P(),
        P("row", "col", None, None, None),
        P(None, "row", "col", None),
        P("row", "col"),
    )
    out_specs = P(None, None, "row", "col")
    return jax.shard_map(body, mesh=mesh, in_specs=in_specs, out_specs=out_specs, check_vma=False)
```

profile of v0, /device:TPU:0, one launch (start us, length us, event | category | flops | bytes accessed | tf_op | source)
XLA Modules:
  0.0 1100.9 jit_solution(9249279486560857298)
XLA Ops:
  7.4 17.9 %all-reduce = s32[16]{0:T(128)S(1)} all-reduce(s32[16]{0:T(128)S(1)} %bitcast_dynamic-update-slice_fusion.2), channel_id=1, replica_groups=mesh['row'=8,'col'=16] {'col'}, use_global_device_ids=true, to_apply=%add | all-reduce | flops 16 | bytes 128
  25.3 19.1 %while.49 = (s32[]{:T(128)}, s32[1]{0:T(128)}, s32[]{:T(128)}, s32[16,1]{0,1:T(1,128)S(1)}, s32[]{:T(128)}) while((s32[]{:T(128)}, s32[1]{0:T(128)}, s32[]{:T(128)}, s32[16,1]{0,1:T(1,128)S(1)}, s32[]{:T(128)}) %tuple.194), condition=%wide.region_1.2_spmd, body=%wide.region_0.1_spmd.sunk | while | flops 5 | bytes 107 | solution.py:25
  69.9 8.3 all-to-all-start.2
  80.7 63.2 %while.52 = (s32[]{:T(128)}, f32[2,2,384,384]{2,3,1,0:T(8,128)}, s32[16,4]{0,1:T(4,128)S(1)}, f32[16,2,2,128,128]{4,3,2,1,0:T(8,128)}, s32[]{:T(128)}) while((s32[]{:T(128)}, f32[2,2,384,384]{2,3,1,0:T(8,128)}, s32[16,4]{0,1:T(4,128)S(1)}, f32[16,2,2,128,128]{4,3,2,1,0:T(8,128)}, s32[]{:T(128)}) %tuple.176), condition=%wide.while_cond.8, body=%wide.while_body.8.sunk | while | flops 2 | bytes 1573497 | solution.py:125
  143.9 5.0 gather_fusion.3
  148.9 4.9 select_bitcast_fusion.1
  154.7 7.7 all-to-all-start
  165.2 48.0 %all-to-all-done = f32[16,1,2,2,128,128]{5,4,3,2,1,0:T(8,128)} async-done(((f32[16,1,2,2,128,128]{5,4,3,2,1,0:T(8,128)}), f32[16,1,2,2,128,128]{5,4,3,2,1,0:T(8,128)}, u32[]{:S(2)}, u32[]{:S(2)}) %all-to-all-start) | async-done | bytes 4194336 | tf_op jit(solution)/shard_map/all_to_all | solution.py:206
  277.8 4.4 gather_fusion.5
  282.2 5.1 fusion.1
  287.3 5.7 all-to-all-start.3
  293.0 50.9 %all-to-all-done.3 = f32[16,1,2,2,128,128]{5,4,3,2,1,0:T(8,128)} async-done(((f32[16,1,2,2,128,128]{5,4,3,2,1,0:T(8,128)}), f32[16,1,2,2,128,128]{5,4,3,2,1,0:T(8,128)}, u32[]{:S(2)}, u32[]{:S(2)}) %all-to-all-start.3) | async-done | bytes 4194336 | tf_op jit(solution)/shard_map/all_to_all | solution.py:234
  344.0 5.0 gather_fusion.6
  349.0 4.9 broadcast_select_fusion.1
  355.4 169.4 %while.50 = (s32[]{:T(128)}, f32[2,2,384,384]{3,2,1,0:T(8,128)}, s32[16]{0:T(128)S(1)}, s32[16]{0:T(128)S(1)}, f32[16,2,2,128,128]{4,3,2,1,0:T(8,128)}, /*index=5*/s32[]{:T(128)}, s32[]{:T(128)}, s32[]{:T(128)}) while((s32[]{:T(128)}, f32[2,2,384,384]{3,2,1,0:T(8,128)}, s32[16]{0:T(128)S(1)}, s32[16]{0:T(128)S(1)}, ...), condition=%wide.region_5.9_spmd, body=%wide.region_4.8_spmd.sunk | while | flops 65544 | bytes 1310913 | solution.py:139
  403.5 4.4 dynamic_update_slice.16
  414.2 4.4 dynamic_update_slice.16
  467.3 4.4 dynamic_update_slice.16
  541.5 6.4 collective-permute-done.6
  547.9 5.4 collective-permute-done.7
  559.1 6.5 scatter-add.26
  567.6 5.0 scatter-add.29
  577.2 5.8 collective-permute-start.8
  584.5 4.5 collective-permute-done.9
  590.2 4.5 collective-permute-start.10
  600.3 5.2 collective-permute-done.11
  610.0 61.7 %while.53 = (s32[]{:T(128)}, f32[2,2,384,384]{2,3,1,0:T(8,128)}, s32[16,4]{0,1:T(4,128)S(1)}, f32[16,2,2,128,128]{4,3,2,1,0:T(8,128)}, s32[]{:T(128)}) while((s32[]{:T(128)}, f32[2,2,384,384]{2,3,1,0:T(8,128)}, s32[16,4]{0,1:T(4,128)S(1)}, f32[16,2,2,128,128]{4,3,2,1,0:T(8,128)}, s32[]{:T(128)}) %tuple.191), condition=%wide.while_cond.9, body=%wide.while_body.9.sunk | while | flops 2 | bytes 1573497 | solution.py:125
  671.7 5.1 gather_fusion.7
  679.5 54.8 %all_to_all.34 = f32[16,1,2,2,128,128]{5,4,3,2,1,0:T(8,128)} all-to-all(f32[16,1,2,2,128,128]{5,4,3,2,1,0:T(8,128)S(1)} %select_bitcast_fusion), channel_id=1, replica_groups=mesh['row'=8,'col'=16] {'col'}, dimensions={0} | all-to-all | bytes 8388608 | tf_op jit(solution)/shard_map/all_to_all | solution.py:222
  799.9 5.1 fusion
  805.0 4.7 all-to-all-start.5
  809.8 47.4 %all-to-all-done.5 = f32[16,1,2,2,128,128]{5,4,3,2,1,0:T(8,128)} async-done(((f32[16,1,2,2,128,128]{5,4,3,2,1,0:T(8,128)}), f32[16,1,2,2,128,128]{5,4,3,2,1,0:T(8,128)}, u32[]{:S(2)}, u32[]{:S(2)}) %all-to-all-start.5) | async-done | bytes 4194336 | tf_op jit(solution)/shard_map/all_to_all | solution.py:234
  857.1 5.0 gather_fusion.10
  862.1 4.9 broadcast_select_fusion
  868.6 161.3 %while.51 = (s32[]{:T(128)}, f32[2,2,384,384]{3,2,1,0:T(8,128)}, s32[16]{0:T(128)S(1)}, s32[16]{0:T(128)S(1)}, f32[16,2,2,128,128]{4,3,2,1,0:T(8,128)}, /*index=5*/s32[]{:T(128)}, s32[]{:T(128)}, s32[]{:T(128)}) while((s32[]{:T(128)}, f32[2,2,384,384]{3,2,1,0:T(8,128)}, s32[16]{0:T(128)S(1)}, s32[16]{0:T(128)S(1)}, ...), condition=%wide.region_7.11_spmd, body=%wide.region_6.10_spmd.sunk | while | flops 65544 | bytes 1310913 | solution.py:139
  914.1 4.4 dynamic_update_slice.17
  924.3 4.4 dynamic_update_slice.17
  934.5 4.4 dynamic_update_slice.17
  954.8 4.4 dynamic_update_slice.17
  974.8 4.4 dynamic_update_slice.17
  985.1 4.4 dynamic_update_slice.17
  1015.3 4.4 dynamic_update_slice.17
  1031.0 11.8 %collective-permute-start.12 = (f32[2,2,64,384]{3,2,1,0:T(8,128)S(1)}, f32[2,2,64,384]{3,2,1,0:T(8,128)S(1)}, u32[]{:S(2)}, u32[]{:S(2)}) collective-permute-start(f32[2,2,64,384]{3,2,1,0:T(8,128)S(1)} %get-tuple-element.484), channel_id=1, source_target_pairs={{0,16},{16,32},{32,48},{48,64},{64,80},{80,96},{96,112},{1,17},{17... | collective-permute-start | bytes 1179656 | tf_op jit(solution)/shard_map/ppermute | solution.py:36
  1047.5 12.2 %collective-permute-done.13 = f32[2,2,64,384]{3,2,1,0:T(8,128)S(1)} collective-permute-done((f32[2,2,64,384]{3,2,1,0:T(8,128)S(1)}, f32[2,2,64,384]{3,2,1,0:T(8,128)S(1)}, u32[]{:S(2)}, u32[]{:S(2)}) %collective-permute-start.13) | collective-permute-done | bytes 393248 | tf_op jit(solution)/shard_map/ppermute | solution.py:38
  1065.0 5.9 collective-permute-done.14
  1070.9 4.7 collective-permute-done.15
  1081.5 6.5 scatter-add.34
  1089.9 5.0 scatter-add.35
  (535 shorter events, 544.8 us)
Async XLA Ops:
  0.0 56.8 %copy-start = (f32[1,1,16,128,128]{4,3,2,1,0:T(8,128)S(1)}, f32[1,1,16,128,128]{4,3,2,1,0:T(8,128)}, u32[]{:S(2)}) copy-start(f32[1,1,16,128,128]{4,3,2,1,0:T(8,128)} %param.35) | copy-start | bytes 3145732
  0.0 6.0 copy-start.16
  0.0 49.3 %copy-start.14 = (s32[2,1,1,16]{3,2,1,0:T(1,128)S(1)}, s32[2,1,1,16]{3,2,1,0:T(1,128)}, u32[]{:S(2)}) copy-start(s32[2,1,1,16]{3,2,1,0:T(1,128)} %param.36) | copy-start | bytes 388
  2.8 47.1 %collective-permute-start = (f32[2,2,64,256]{2,3,1,0:T(8,128)}, f32[2,2,64,256]{2,3,1,0:T(8,128)S(1)}, u32[]{:S(2)}, u32[]{:S(2)}) collective-permute-start(f32[2,2,64,256]{2,3,1,0:T(8,128)} %get-tuple-element.510), channel_id=1, source_target_pairs={{0,16},{16,32},{32,48},{48,64},{64,80},{80,96},{96,112},{1,17},{17... | collective-permute-start | bytes 786440 | tf_op jit(solution)/shard_map/ppermute | solution.py:36
  4.1 45.8 %collective-permute-start.1 = (f32[2,2,64,256]{2,3,1,0:T(8,128)}, f32[2,2,64,256]{2,3,1,0:T(8,128)S(1)}, u32[]{:S(2)}, u32[]{:S(2)}) collective-permute-start(f32[2,2,64,256]{2,3,1,0:T(8,128)} %get-tuple-element.511), channel_id=1, source_target_pairs={{16,0},{32,16},{48,32},{64,48},{80,64},{96,80},{112,96},{17,1},{33... | collective-permute-start | bytes 786440 | tf_op jit(solution)/shard_map/ppermute | solution.py:38
  44.5 6.7 copy-start.12
  45.9 24.0 %all-to-all-start.1 = ((f32[16,1,1]{2,1,0:T(1,128)}), f32[16,1,1]{2,1,0:T(1,128)S(1)}, u32[]{:S(2)}, u32[]{:S(2)}) async-start(f32[16,1,1]{2,1,0:T(1,128)} %copy.547), calls=%async_computation.1 | async-start | bytes 16384 | tf_op jit(solution)/shard_map/all_to_all | solution.py:208
  49.9 6.9 copy-start.8
  49.9 6.9 copy-start.9
  51.2 11.2 %collective-permute-start.2 = (f32[2,2,384,64]{2,3,1,0:T(8,128)}, f32[2,2,384,64]{2,3,1,0:T(8,128)S(1)}, u32[]{:S(2)}, u32[]{:S(2)}) collective-permute-start(f32[2,2,384,64]{2,3,1,0:T(8,128)} %get-tuple-element.494), channel_id=1, source_target_pairs={{0,1},{1,2},{2,3},{3,4},{4,5},{5,6},{6,7},{7,8},{8,9},{9,10},{10,1... | collective-permute-start | bytes 1179656 | tf_op jit(solution)/shard_map/ppermute | solution.py:36
  54.9 11.6 %collective-permute-start.3 = (f32[2,2,384,64]{2,3,1,0:T(8,128)}, f32[2,2,384,64]{2,3,1,0:T(8,128)}, u32[]{:S(2)}, u32[]{:S(2)}) collective-permute-start(f32[2,2,384,64]{2,3,1,0:T(8,128)} %get-tuple-element.495), channel_id=1, source_target_pairs={{1,0},{2,1},{3,2},{4,3},{5,4},{6,5},{7,6},{8,7},{9,8},{10,9},{11,1... | collective-permute-start | bytes 1179656 | tf_op jit(solution)/shard_map/ppermute | solution.py:38
  58.1 85.7 %copy-start.11 = (s32[1024]{0:T(1024)}, s32[1024]{0:T(1024)S(1)}, u32[]{:S(2)}) copy-start(s32[1024]{0:T(1024)S(1)} %pad_clamp_fusion.4) | copy-start | bytes 12292
  69.9 83.9 %all-to-all-start.2 = ((f32[16,1,128,128]{3,2,1,0:T(8,128)}), f32[16,1,128,128]{3,2,1,0:T(8,128)S(1)}, u32[]{:S(2)}, u32[]{:S(2)}) async-start(f32[16,1,128,128]{3,2,1,0:T(8,128)} %bitcast_select_fusion), calls=%async_computation.2 | async-start | bytes 2097152 | tf_op jit(solution)/shard_map/all_to_all | solution.py:207
  143.9 5.0 copy-start.13
  153.8 9.0 copy-start.10
  153.8 1.0 copy-start.7
  154.7 58.5 %all-to-all-start = ((f32[16,1,2,2,128,128]{5,4,3,2,1,0:T(8,128)}), f32[16,1,2,2,128,128]{5,4,3,2,1,0:T(8,128)}, u32[]{:S(2)}, u32[]{:S(2)}) async-start(f32[16,1,2,2,128,128]{5,4,3,2,1,0:T(8,128)} %select_bitcast_fusion.1), calls=%async_computation | async-start | bytes 8388608 | tf_op jit(solution)/shard_map/all_to_all | solution.py:206
  165.2 81.3 %copy-start.5 = (f32[8,128,128]{2,1,0:T(8,128)}, f32[8,128,128]{2,1,0:T(8,128)S(1)}, u32[]{:S(2)}) copy-start(f32[8,128,128]{2,1,0:T(8,128)S(1)} %gather_fusion.2) | copy-start | bytes 1572868
  287.3 5.7 copy-start.15
  287.3 56.7 %all-to-all-start.3 = ((f32[16,1,2,2,128,128]{5,4,3,2,1,0:T(8,128)}), f32[16,1,2,2,128,128]{5,4,3,2,1,0:T(8,128)}, u32[]{:S(2)}, u32[]{:S(2)}) async-start(f32[16,1,2,2,128,128]{5,4,3,2,1,0:T(8,128)} %fusion.1), calls=%async_computation.3 | async-start | bytes 8388608 | tf_op jit(solution)/shard_map/all_to_all | solution.py:234
  526.0 6.4 collective-permute-start.4
  528.1 6.5 collective-permute-start.5
  535.7 17.6 %copy-start.4 = (f32[2,2,64,384]{2,3,1,0:T(8,128)S(1)}, f32[2,2,64,384]{2,3,1,0:T(8,128)}, u32[]{:S(2)}) copy-start(f32[2,2,64,384]{2,3,1,0:T(8,128)} %copy.605) | copy-start | bytes 1179652
  537.4 10.5 collective-permute-start.6
  540.2 13.1 %collective-permute-start.7 = (f32[2,2,512,64]{2,3,1,0:T(8,128)S(1)}, f32[2,2,512,64]{2,3,1,0:T(8,128)S(1)}, u32[]{:S(2)}, u32[]{:S(2)}) collective-permute-start(f32[2,2,512,64]{2,3,1,0:T(8,128)S(1)} %get-tuple-element.475), channel_id=1, source_target_pairs={{1,0},{2,1},{3,2},{4,3},{5,4},{6,5},{7,6},{8,7},{9,8},{10,9},{11,1... | collective-permute-start | bytes 1572872 | tf_op jit(solution)/shard_map/ppermute | solution.py:38
  556.1 2.9 copy-start.3
  577.2 7.3 collective-permute-start.8
  583.0 6.0 collective-permute-start.9
  590.2 10.1 collective-permute-start.10
  594.7 10.7 collective-permute-start.11
  761.5 5.9 copy-start.6
  805.0 52.1 %all-to-all-start.5 = ((f32[16,1,2,2,128,128]{5,4,3,2,1,0:T(8,128)}), f32[16,1,2,2,128,128]{5,4,3,2,1,0:T(8,128)}, u32[]{:S(2)}, u32[]{:S(2)}) async-start(f32[16,1,2,2,128,128]{5,4,3,2,1,0:T(8,128)} %fusion), calls=%async_computation.5 | async-start | bytes 8388608 | tf_op jit(solution)/shard_map/all_to_all | solution.py:234
  1031.0 16.2 %collective-permute-start.12 = (f32[2,2,64,384]{3,2,1,0:T(8,128)S(1)}, f32[2,2,64,384]{3,2,1,0:T(8,128)S(1)}, u32[]{:S(2)}, u32[]{:S(2)}) collective-permute-start(f32[2,2,64,384]{3,2,1,0:T(8,128)S(1)} %get-tuple-element.484), channel_id=1, source_target_pairs={{0,16},{16,32},{32,48},{48,64},{64,80},{80,96},{96,112},{1,17},{17... | collective-permute-start | bytes 1179656 | tf_op jit(solution)/shard_map/ppermute | solution.py:36
  1042.8 16.9 %collective-permute-start.13 = (f32[2,2,64,384]{3,2,1,0:T(8,128)S(1)}, f32[2,2,64,384]{3,2,1,0:T(8,128)S(1)}, u32[]{:S(2)}, u32[]{:S(2)}) collective-permute-start(f32[2,2,64,384]{3,2,1,0:T(8,128)S(1)} %get-tuple-element.485), channel_id=1, source_target_pairs={{16,0},{32,16},{48,32},{64,48},{80,64},{96,80},{112,96},{17,1},{33... | collective-permute-start | bytes 1179656 | tf_op jit(solution)/shard_map/ppermute | solution.py:38
  1061.5 9.4 collective-permute-start.14
  1063.7 11.9 %collective-permute-start.15 = (f32[2,2,512,64]{2,3,1,0:T(8,128)S(1)}, f32[2,2,512,64]{2,3,1,0:T(8,128)S(1)}, u32[]{:S(2)}, u32[]{:S(2)}) collective-permute-start(f32[2,2,512,64]{2,3,1,0:T(8,128)S(1)} %get-tuple-element.473), channel_id=1, source_target_pairs={{1,0},{2,1},{3,2},{4,3},{5,4},{6,5},{7,6},{8,7},{9,8},{10,9},{11,1... | collective-permute-start | bytes 1572872 | tf_op jit(solution)/shard_map/ppermute | solution.py:38
  1078.4 2.9 copy-start.2
  1096.7 4.0 copy-start.1
where the time goes:
time: 1120 us; the launch traced here: 1100 us
  local copies, waits for them, and re-layouts  406 us (36%)
  waiting for transfers between devices  203 us (18%)
  loops' own time  126 us (11%)
  matrix products  112 us (10%)
  other arithmetic  105 us (9%)
  starting transfers between devices  74.3 us (7%)
  blocking collectives  72.7 us (6%)
    dynamic_update_slice x32, local copies, waits for them, and re-layouts, add_one(): lax.dynamic_update_slice(accumulator, current_block + gradients[item], co...  136 us
    gather x160, local copies, waits for them, and re-layouts  124 us
    another operation x2, loops' own time, place_patches(): lax.fori_loop(0, gradients.shape[0], add_one, jnp.zeros(ext_shape, jnp.fl...  115 us
    all_to_all x2, waiting for transfers between devices, body(): lax.all_to_all(returned.reshape(col_count, per_peer, layers, 2, frame_siz...  98.3 us
    dot_general x48, matrix products, apply_left(): return jnp.einsum('jk,bkl->bjl', matrix, values, precision=highest)  57.1 us
    dot_general x48, matrix products, apply_right(): return jnp.einsum('bjk,kl->bjl', values, matrix, precision=highest)  55.4 us
    all_to_all x1, blocking collectives, body(): lax.all_to_all(outgoing, 'col', split_axis=0, concat_axis=0, tiled=True)  54.8 us
    all_to_all x1, waiting for transfers between devices, body(): lax.all_to_all(outgoing, 'col', split_axis=0, concat_axis=0, tiled=True)  48 us
  transfers between devices with their start and end apart: 21, of which 15 were waited for; matrix products, arithmetic and copies ran while one was open for 10% of the time, Pallas kernels for 0%

commit v1 on v0

v1 whole, which is shorter than its diff:
```python
import functools
import math

import jax
import jax.numpy as jnp
import numpy as np
from jax import lax
from jax.experimental import pallas as pl
from jax.experimental.pallas import tpu as pltpu
from jax.sharding import PartitionSpec as P

ITERS = 2
MESH = pl.DeviceIdType.MESH
F32 = jnp.float32
BF16 = jnp.bfloat16

modulus_offset = 0.5
fresnel_scale = 0.9

N = 128
T = 256
E = T + N
HALF = N // 2
LANES = E // N
SLOTS = 16
GROUP = 4
GROWS = N + 16


def tables():
    positions = np.arange(N)
    frequency = np.where(positions < N // 2, positions, positions - N).astype(np.float64)
    angle = -2.0 * math.pi / N * (np.outer(positions, positions) % N)
    dft = (np.cos(angle) + 1j * np.sin(angle)) / math.sqrt(N)
    phase = math.pi * fresnel_scale * frequency**2 / N
    spread = np.conj(dft) @ (np.exp(1j * phase)[:, None] * dft)
    spread = 0.5 * (spread + spread.T)
    made = []
    for matrix in (spread, dft):
        left = np.block([[matrix.real, -matrix.imag], [matrix.imag, matrix.real]])
        for form in (left, left.T):
            high = form.astype(np.float32).astype(BF16)
            low = (form - high.astype(np.float64)).astype(np.float32).astype(BF16)
            made += [high, low]
    return np.stack(made)


def split(value):
    high = value.astype(BF16)
    return high, (value - high.astype(F32)).astype(BF16)


def dot(a, b):
    return jnp.dot(a, b, preferred_element_type=F32)


def kernel(
    rows_n, cols_n,
    pos_ref, count_ref, obj_ref, probe_ref, amps_ref, tab_ref,
    out_ref,
    ext0, ext1, acc0, acc1, inc_ref, lay_ref, grad_ref,
    halo_src, halo_dst, up_ref, down_ref, left_ref, right_ref,
    fin_up, fin_down, fin_src, fin_dst,
    send_sem, recv_sem,
):
    row, col = lax.axis_index("row"), lax.axis_index("col")
    up = (lax.rem(row + rows_n - 1, rows_n), col)
    down = (lax.rem(row + 1, rows_n), col)
    left = (row, lax.rem(col + cols_n - 1, cols_n))
    right = (row, lax.rem(col + 1, cols_n))
    has_up, has_down = row > 0, row < rows_n - 1
    has_left, has_right = col > 0, col < cols_n - 1
    ext, acc = (ext0, ext1), (acc0, acc1)
    used = [0]

    barrier = pltpu.get_barrier_semaphore()
    for device in (up, down, left, right):
        pl.semaphore_signal(barrier, inc=1, device_id=device, device_id_type=MESH)

    def copy(source, target, device):
        index = used[0]
        used[0] += 1
        made = pltpu.make_async_remote_copy(
            src_ref=source, dst_ref=target, send_sem=send_sem.at[index],
            recv_sem=recv_sem.at[index], device_id=device, device_id_type=MESH,
        )
        made.start()
        return made

    def wait(copies):
        for made in copies:
            made.wait()

    lane = lax.broadcasted_iota(jnp.int32, (N, N), 1)
    low = lane < HALF

    def swap(value):
        return pltpu.roll(value, HALF, 1)

    low_t = lax.broadcasted_iota(jnp.int32, (T, N), 1) < HALF
    for s in range(2):
        first = [obj_ref[s, c, :, 0:N] for c in range(2)]
        last = [obj_ref[s, c, :, N : 2 * N] for c in range(2)]
        halo_src[s, 0] = jnp.where(low_t, first[1], swap(first[0]))
        halo_src[s, 1] = jnp.where(low_t, swap(last[0]), last[1])

    pl.semaphore_wait(barrier, 4)
    side = [
        [copy(halo_src.at[s, 0], halo_dst.at[s, 1], left), copy(halo_src.at[s, 1], halo_dst.at[s, 0], right)]
        for s in range(2)
    ]

    for s in range(2):
        for c in range(2):
            first, last = swap(obj_ref[s, c, :, 0:N]), swap(obj_ref[s, c, :, N : 2 * N])
            ext[s][c, 1, HALF : HALF + T, :] = jnp.where(low_t, first, last)

    def clear(k, carry):
        for c in range(2):
            for t in range(LANES):
                grad_ref[k, c, t, 0:8, :] = jnp.zeros((8, N), F32)
                grad_ref[k, c, t, GROWS - 8 : GROWS, :] = jnp.zeros((8, N), F32)
        return carry

    lax.fori_loop(0, SLOTS, clear, 0)

    edge = []
    for s in range(2):
        wait(side[s])
        from_left = jnp.where(has_left, halo_dst[s, 0], 0.0)
        from_right = jnp.where(has_right, halo_dst[s, 1], 0.0)
        for c in range(2):
            first, last = swap(obj_ref[s, c, :, 0:N]), swap(obj_ref[s, c, :, N : 2 * N])
            ext[s][c, 0, HALF : HALF + T, :] = jnp.where(low_t, from_left if c == 0 else swap(from_left), first)
            ext[s][c, 2, HALF : HALF + T, :] = jnp.where(low_t, last, from_right if c == 0 else swap(from_right))
        edge.append([
            copy(ext[s].at[:, :, HALF : 2 * HALF, :], ext[s].at[:, :, E - HALF : E, :], up),
            copy(ext[s].at[:, :, T : T + HALF, :], ext[s].at[:, :, 0:HALF, :], down),
        ])

    def border(s):
        wait(edge[s])
        ext[s][:, :, 0:HALF, :] = jnp.where(has_up, ext[s][:, :, 0:HALF, :], 0.0)
        ext[s][:, :, E - HALF : E, :] = jnp.where(has_down, ext[s][:, :, E - HALF : E, :], 0.0)

    def place(k):
        at_row, at_col = lax.rem(pos_ref[0, k], T), lax.rem(pos_ref[1, k], T)
        return at_row, at_col // N, at_col % N

    def patch(s, k):
        at_row, at_lane, shift = place(k)
        back = (N - shift) % N
        parts = []
        for c in range(2):
            here = ext[s][c, at_lane, pl.ds(at_row, N), :]
            after = ext[s][c, at_lane + 1, pl.ds(at_row, N), :]
            parts.append(pltpu.roll(jnp.where(lane >= shift, here, after), back, 1))
        return parts

    def put(k, parts):
        at_row, at_lane, shift = place(k)
        live = (k < count_ref[0, 0]).astype(F32)
        second = live * at_lane.astype(F32)
        first = live - second
        for c in range(2):
            moved = pltpu.roll(parts[c], shift, 1)
            here = jnp.where(lane >= shift, moved, 0.0)
            after = jnp.where(lane >= shift, 0.0, moved)
            grad_ref[k, c, 0, 8 : 8 + N, :] = here * first
            grad_ref[k, c, 1, 8 : 8 + N, :] = here * second + after * first
            grad_ref[k, c, 2, 8 : 8 + N, :] = after * second

    def apply(which, waves):
        high_l, low_l = tab_ref[2 * which], tab_ref[2 * which + 1]
        other = which ^ 1
        high_r, low_r = tab_ref[2 * other], tab_ref[2 * other + 1]
        (re_a, im_a), (re_b, im_b) = waves
        value = jnp.concatenate(
            [jnp.concatenate([re_a, re_b], axis=1), jnp.concatenate([im_a, im_b], axis=1)], axis=0
        )
        high, low_part = split(value)
        mid = dot(high_l, high) + dot(high_l, low_part) + dot(low_l, high)
        value = jnp.concatenate(
            [
                jnp.concatenate([mid[:N, :N], mid[N:, :N]], axis=1),
                jnp.concatenate([mid[:N, N:], mid[N:, N:]], axis=1),
            ],
            axis=0,
        )
        high, low_part = split(value)
        done = dot(high, high_r) + dot(low_part, high_r) + dot(high, low_r)
        return (done[:N, :N], done[:N, N:]), (done[N:, :N], done[N:, N:])

    def product(a, b):
        return a[0] * b[0] - a[1] * b[1], a[0] * b[1] + a[1] * b[0]

    def product_conj(a, b):
        return a[0] * b[0] + a[1] * b[1], a[0] * b[1] - a[1] * b[0]

    SPREAD, SPREAD_ADJ, DFT, DFT_INV = 0, 1, 2, 3

    def loop(stage, start, stop):
        def step(g, carry):
            for pair in range(GROUP // 2):
                stage([g * GROUP + 2 * pair, g * GROUP + 2 * pair + 1])
            return carry

        lax.fori_loop(start // GROUP, stop // GROUP, step, 0)

    def ahead(slots):
        illum = (probe_ref[0], probe_ref[1])
        waves = apply(SPREAD, [product(illum, patch(0, k)) for k in slots])
        for k, wave in zip(slots, waves):
            inc_ref[k, 0], inc_ref[k, 1] = wave

    def detect(slots):
        exits = []
        for k in slots:
            layer = patch(1, k)
            lay_ref[k, 0], lay_ref[k, 1] = layer
            exits.append(product((inc_ref[k, 0], inc_ref[k, 1]), layer))
        residuals = []
        for k, (re, im) in zip(slots, apply(DFT, exits)):
            factor = 1.0 - amps_ref[k] / jnp.sqrt(re * re + im * im + modulus_offset)
            residuals.append((re * factor, im * factor))
        for k, back in zip(slots, apply(DFT_INV, residuals)):
            put(k, product_conj((inc_ref[k, 0], inc_ref[k, 1]), back))
            lay_ref[k, 0], lay_ref[k, 1] = product_conj((lay_ref[k, 0], lay_ref[k, 1]), back)

    def behind(slots):
        illum = (probe_ref[0], probe_ref[1])
        for k, back in zip(slots, apply(SPREAD_ADJ, [(lay_ref[k, 0], lay_ref[k, 1]) for k in slots])):
            put(k, product_conj(illum, back))

    def gather(s):
        def step(block, carry):
            at = block * 8
            sums = [jnp.zeros((8, N), F32)] * (2 * LANES)
            for k in range(SLOTS):
                from_row = jnp.clip(at - lax.rem(pos_ref[0, k], T) + 8, 0, GROWS - 8)
                sums = [
                    total + grad_ref[k, i // LANES, i % LANES, pl.ds(from_row, 8), :]
                    for i, total in enumerate(sums)
                ]
            for i, total in enumerate(sums):
                acc[s][i // LANES, i % LANES, pl.ds(pl.multiple_of(at, 8), 8), :] = total
            return carry

        lax.fori_loop(0, E // 8, step, 0)

    def mid_start(s):
        rows = [
            copy(acc[s].at[:, :, 0:N, :], down_ref.at[s], up),
            copy(acc[s].at[:, :, T:E, :], up_ref.at[s], down),
        ]
        cols = [
            copy(acc[s].at[:, 0, N:T, :], right_ref.at[s, :, N:T, :], left),
            copy(acc[s].at[:, 2, N:T, :], left_ref.at[s, :, N:T, :], right),
        ]
        return rows, cols

    def mid_next(s, copies):
        rows, cols = copies
        wait(rows)
        acc[s][:, :, 0:N, :] = acc[s][:, :, 0:N, :] + jnp.where(has_up, up_ref[s], 0.0)
        acc[s][:, :, T:E, :] = acc[s][:, :, T:E, :] + jnp.where(has_down, down_ref[s], 0.0)
        for part in (slice(0, N), slice(T, E)):
            cols = cols + [
                copy(acc[s].at[:, 0, part, :], right_ref.at[s, :, part, :], left),
                copy(acc[s].at[:, 2, part, :], left_ref.at[s, :, part, :], right),
            ]
        return cols

    def mid_end(s, cols):
        wait(cols)
        inside = ((low == False) | has_left, (low == low), low | has_right)
        for c in range(2):
            for t in range(LANES):
                for b in range(LANES):
                    part = slice(b * N, b * N + N)
                    value = ext[s][c, t, part, :] - acc[s][c, t, part, :]
                    if t == 0:
                        value = value - jnp.where(has_left, left_ref[s, c, part, :], 0.0)
                    if t == 2:
                        value = value - jnp.where(has_right, right_ref[s, c, part, :], 0.0)
                    if t != 1:
                        value = jnp.where(inside[t], value, 0.0)
                    if b != 1:
                        line = lax.broadcasted_iota(jnp.int32, (N, N), 0)
                        keep = ((line >= HALF) | has_up) if b == 0 else ((line < HALF) | has_down)
                        value = jnp.where(keep, value, 0.0)
                    ext[s][c, t, part, :] = value

    def fin_start(s):
        return [
            copy(acc[s].at[:, :, 0:HALF, :], fin_down.at[s], up),
            copy(acc[s].at[:, :, E - HALF : E, :], fin_up.at[s], down),
        ]

    def fin_next(s, rows):
        wait(rows)
        head, tail = slice(HALF, N), slice(T, T + HALF)
        acc[s][:, :, head, :] = acc[s][:, :, head, :] + jnp.where(has_up, fin_up[s], 0.0)
        acc[s][:, :, tail, :] = acc[s][:, :, tail, :] + jnp.where(has_down, fin_down[s], 0.0)
        own = slice(HALF, HALF + T)
        fin_src[s, 0] = jnp.where(low_t, acc[s][0, 0, own, :], swap(acc[s][1, 0, own, :]))
        fin_src[s, 1] = jnp.where(low_t, swap(acc[s][1, 2, own, :]), acc[s][0, 2, own, :])
        return [copy(fin_src.at[s, 0], fin_dst.at[s, 1], left), copy(fin_src.at[s, 1], fin_dst.at[s, 0], right)]

    def fin_end(s, cols):
        wait(cols)
        own = slice(HALF, HALF + T)
        from_left = jnp.where(has_left, fin_dst[s, 0], 0.0)
        from_right = jnp.where(has_right, fin_dst[s, 1], 0.0)
        for c in range(2):
            mine = [ext[s][c, t, own, :] - acc[s][c, t, own, :] for t in range(LANES)]
            begin = swap(mine[0] - (from_left if c == 0 else swap(from_left)))
            middle = swap(mine[1])
            end = swap(mine[2] - (from_right if c == 0 else swap(from_right)))
            out_ref[s, c, :, 0:N] = jnp.where(low_t, begin, middle)
            out_ref[s, c, :, N : 2 * N] = jnp.where(low_t, middle, end)

    border(0)
    loop(ahead, 0, SLOTS)
    border(1)
    loop(detect, 0, SLOTS)
    gather(1)
    one = mid_start(1)
    loop(behind, 0, SLOTS // 2)
    one = mid_next(1, one)
    loop(behind, SLOTS // 2, SLOTS)
    gather(0)
    mid_end(0, mid_next(0, mid_start(0)))

    loop(ahead, 0, SLOTS)
    mid_end(1, one)
    loop(detect, 0, SLOTS)
    gather(1)
    one = fin_start(1)
    loop(behind, 0, SLOTS // 2)
    one = fin_next(1, one)
    loop(behind, SLOTS // 2, SLOTS)
    gather(0)
    zero = fin_next(0, fin_start(0))
    fin_end(1, one)
    fin_end(0, zero)


COPIES = 32


def solution(mesh):
    rows_n, cols_n = mesh.shape["row"], mesh.shape["col"]
    vmem = pl.BlockSpec(memory_space=pltpu.VMEM)
    smem = pl.BlockSpec(memory_space=pltpu.SMEM)

    def body(object_slices, probe, amplitudes, scan_pos, scan_count):
        tab = jnp.asarray(tables())
        call = pl.pallas_call(
            functools.partial(kernel, rows_n, cols_n),
            out_shape=jax.ShapeDtypeStruct(object_slices.shape, F32),
            in_specs=[smem, smem, vmem, vmem, vmem, vmem],
            out_specs=vmem,
            scratch_shapes=[
                pltpu.VMEM((2, LANES, E, N), F32),
                pltpu.VMEM((2, LANES, E, N), F32),
                pltpu.VMEM((2, LANES, E, N), F32),
                pltpu.VMEM((2, LANES, E, N), F32),
                pltpu.VMEM((SLOTS, 2, N, N), F32),
                pltpu.VMEM((SLOTS, 2, N, N), F32),
                pltpu.VMEM((SLOTS, 2, LANES, GROWS, N), F32),
                pltpu.VMEM((2, 2, T, N), F32),
                pltpu.VMEM((2, 2, T, N), F32),
                pltpu.VMEM((2, 2, LANES, N, N), F32),
                pltpu.VMEM((2, 2, LANES, N, N), F32),
                pltpu.VMEM((2, 2, E, N), F32),
                pltpu.VMEM((2, 2, E, N), F32),
                pltpu.VMEM((2, 2, LANES, HALF, N), F32),
                pltpu.VMEM((2, 2, LANES, HALF, N), F32),
                pltpu.VMEM((2, 2, T, N), F32),
                pltpu.VMEM((2, 2, T, N), F32),
                pltpu.SemaphoreType.DMA((COPIES,)),
                pltpu.SemaphoreType.DMA((COPIES,)),
            ],
            compiler_params=pltpu.CompilerParams(
                collective_id=0, has_side_effects=True, vmem_limit_bytes=56 * 2**20
            ),
        )
        return call(
            scan_pos.reshape(2, SLOTS), scan_count, object_slices, probe,
            amplitudes.reshape(SLOTS, N, N), tab,
        )

    in_specs = (
        P(None, None, "row", "col"),
        P(),
        P("row", "col", None, None, None),
        P(None, "row", "col", None),
        P("row", "col"),
    )
    out_specs = P(None, None, "row", "col")
    return jax.shard_map(body, mesh=mesh, in_specs=in_specs, out_specs=out_specs, check_vma=False)
```

time: 1120 us -> 106 us (0.09); the launches traced: 1100 us -> 106 us
  local copies, waits for them, and re-layouts: 406 us -> 2.29 us
  waiting for transfers between devices: 203 us -> 0 us
  loops' own time: 126 us -> 0 us
  matrix products: 112 us -> 0 us
  other arithmetic: 105 us -> 0 us
  Pallas kernels: 0 us -> 103 us
  starting transfers between devices: 74.3 us -> 0 us
  blocking collectives: 72.7 us -> 0 us
    gather x171 -> x0, local copies, waits for them, and re-layouts: 163 us -> none
    all_to_all x5 -> x0, waiting for transfers between devices: 146 us -> none  [the longest x2 98.3 us: body(): lax.all_to_all(returned.reshape(col_count, per_peer, layers, 2, frame_siz...]
    dynamic_update_slice x32 -> x0, local copies, waits for them, and re-layouts: 136 us -> none  [add_one(): lax.dynamic_update_slice(accumulator, current_block + gradients[item], co...]
    another operation x5 -> x0, loops' own time: 126 us -> none  [the longest x2 115 us: place_patches(): lax.fori_loop(0, gradients.shape[0], add_one, jnp.zeros(ext_shape, jnp.fl...]
    dot_general x96 -> x0, matrix products: 112 us -> none  [the longest x48 57.1 us: apply_left(): return jnp.einsum('jk,bkl->bjl', matrix, values, precision=highest)]
    pallas_call x0 -> x1, Pallas kernels: none -> 103 us  [body(): call(scan_pos.reshape(2, SLOTS), scan_count, object_slices, probe, amplit...]
    ppermute x16 -> x0, waiting for transfers between devices: 56.2 us -> none  [the longest x8 37 us: with_halo(): lax.ppermute(head, axis, [((i + 1) % count, i) for i in range(ends)])]
    all_to_all x1 -> x0, blocking collectives: 54.8 us -> none  [body(): lax.all_to_all(outgoing, 'col', split_axis=0, concat_axis=0, tiled=True)]
  transfers between devices with their start and end apart: 21 -> 0, of which waited for: 15 -> 0; matrix products, arithmetic and copies ran while one was open for 10% -> 0% of each run, Pallas kernels for 0% -> 0%
where the time goes in v1:
time: 106 us
  Pallas kernels  103 us (97%)
  local copies, waits for them, and re-layouts  2.29 us (2%)
    pallas_call x1, Pallas kernels, body(): call(scan_pos.reshape(2, SLOTS), scan_count, object_slices, probe, amplit...  103 us
    unnamed x1, local copies, waits for them, and re-layouts  2.29 us

profile of v1, /device:TPU:0, one launch (start us, length us, event | category | flops | bytes accessed | tf_op | source)
XLA Modules:
  0.0 105.7 jit_solution(15138048924029652118)
XLA Ops:
  0.7 102.8 %shard_map.64 = f32[2,2,256,256]{3,2,1,0:T(8,128)} custom-call(s32[2,16]{1,0:T(2,128)} %bitcast.3, s32[1,1]{1,0:T(1,128)S(6)} %copy.8.count_ref, f32[2,2,256,256]{3,2,1,0:T(8,128)} %obj_ref.1, f32[2,128,128]{2,1,0:T(8,128)} %probe_ref.1, f32[16,128,128]{2,1,0:T(8,128)} %bitcast.2, bf16[8,256,256]{2,1,0:T(8,128)(2,1)} %constant.2.clone.tab_ref), custom_call_target="tpu_custom_call" | custom-call | tf_op jit(solution)/shard_map/pallas_call | solution.py:389
  103.5 2.3 %copy.9 = f32[2,2,256,256]{3,2,1,0:T(8,128)} copy(f32[2,2,256,256]{3,2,1,0:T(8,128)} %shard_map.64) | data formatting | bytes 2097152

commit v2 on v1

--- a/solution.py
+++ b/solution.py
@@ -23,8 +23,9 @@
 HALF = N // 2
 LANES = E // N
 SLOTS = 16
-GROUP = 4
-GROWS = N + 16
+GROUP = 8
+STRIP = 32
+GROWS = N + 2 * STRIP
 
 
 def tables():
@@ -58,7 +59,7 @@
     rows_n, cols_n,
     pos_ref, count_ref, obj_ref, probe_ref, amps_ref, tab_ref,
     out_ref,
-    ext0, ext1, acc0, acc1, inc_ref, lay_ref, grad_ref,
+    ext0, ext1, acc0, acc1, inc_ref, lay_ref, grad_ref, mask_ref,
     halo_src, halo_dst, up_ref, down_ref, left_ref, right_ref,
     fin_up, fin_down, fin_src, fin_dst,
     send_sem, recv_sem,
@@ -115,14 +116,25 @@
             first, last = swap(obj_ref[s, c, :, 0:N]), swap(obj_ref[s, c, :, N : 2 * N])
             ext[s][c, 1, HALF : HALF + T, :] = jnp.where(low_t, first, last)
 
-    def clear(k, carry):
-        for c in range(2):
-            for t in range(LANES):
-                grad_ref[k, c, t, 0:8, :] = jnp.zeros((8, N), F32)
-                grad_ref[k, c, t, GROWS - 8 : GROWS, :] = jnp.zeros((8, N), F32)
+    def place(k):
+        at_row, at_col = lax.rem(pos_ref[0, k], T), lax.rem(pos_ref[1, k], T)
+        return at_row, at_col // N, at_col % N
+
+    def prepare(k, carry):
+        _, at_lane, shift = place(k)
+        live = (k < count_ref[0, 0]).astype(F32)
+        second = live * at_lane.astype(F32)
+        first = live - second
+        upper = (lax.broadcasted_iota(jnp.int32, (8, N), 1) >= shift).astype(F32)
+        mask_ref[k, 0] = upper * first
+        mask_ref[k, 1] = upper * second + (1.0 - upper) * first
+        mask_ref[k, 2] = (1.0 - upper) * second
+        for c in range(2):
+            grad_ref[k, c, 0:STRIP, :] = jnp.zeros((STRIP, N), F32)
+            grad_ref[k, c, GROWS - STRIP : GROWS, :] = jnp.zeros((STRIP, N), F32)
         return carry
 
-    lax.fori_loop(0, SLOTS, clear, 0)
+    lax.fori_loop(0, SLOTS, prepare, 0)
 
     edge = []
     for s in range(2):
@@ -143,10 +155,6 @@
         ext[s][:, :, 0:HALF, :] = jnp.where(has_up, ext[s][:, :, 0:HALF, :], 0.0)
         ext[s][:, :, E - HALF : E, :] = jnp.where(has_down, ext[s][:, :, E - HALF : E, :], 0.0)
 
-    def place(k):
-        at_row, at_col = lax.rem(pos_ref[0, k], T), lax.rem(pos_ref[1, k], T)
-        return at_row, at_col // N, at_col % N
-
     def patch(s, k):
         at_row, at_lane, shift = place(k)
         back = (N - shift) % N
@@ -158,38 +166,27 @@
         return parts
 
     def put(k, parts):
-        at_row, at_lane, shift = place(k)
-        live = (k < count_ref[0, 0]).astype(F32)
-        second = live * at_lane.astype(F32)
-        first = live - second
-        for c in range(2):
-            moved = pltpu.roll(parts[c], shift, 1)
-            here = jnp.where(lane >= shift, moved, 0.0)
-            after = jnp.where(lane >= shift, 0.0, moved)
-            grad_ref[k, c, 0, 8 : 8 + N, :] = here * first
-            grad_ref[k, c, 1, 8 : 8 + N, :] = here * second + after * first
-            grad_ref[k, c, 2, 8 : 8 + N, :] = after * second
+        _, _, shift = place(k)
+        for c in range(2):
+            grad_ref[k, c, STRIP : STRIP + N, :] = pltpu.roll(parts[c], shift, 1)
+
+    def tall(parts):
+        return jnp.concatenate(parts, axis=0)
+
+    def wide(parts):
+        return jnp.concatenate(parts, axis=1)
 
     def apply(which, waves):
         high_l, low_l = tab_ref[2 * which], tab_ref[2 * which + 1]
         other = which ^ 1
         high_r, low_r = tab_ref[2 * other], tab_ref[2 * other + 1]
-        (re_a, im_a), (re_b, im_b) = waves
-        value = jnp.concatenate(
-            [jnp.concatenate([re_a, re_b], axis=1), jnp.concatenate([im_a, im_b], axis=1)], axis=0
+        high, low_part = split(tall([wide([wave[c] for wave in waves]) for c in range(2)]))
+        mid = dot(wide([high_l, high_l, low_l]), tall([high, low_part, high]))
+        high, low_part = split(
+            tall([wide([mid[:N, i * N : i * N + N], mid[N:, i * N : i * N + N]]) for i in range(len(waves))])
         )
-        high, low_part = split(value)
-        mid = dot(high_l, high) + dot(high_l, low_part) + dot(low_l, high)
-        value = jnp.concatenate(
-            [
-                jnp.concatenate([mid[:N, :N], mid[N:, :N]], axis=1),
-                jnp.concatenate([mid[:N, N:], mid[N:, N:]], axis=1),
-            ],
-            axis=0,
-        )
-        high, low_part = split(value)
-        done = dot(high, high_r) + dot(low_part, high_r) + dot(high, low_r)
-        return (done[:N, :N], done[:N, N:]), (done[N:, :N], done[N:, N:])
+        done = dot(wide([high, low_part, high]), tall([high_r, high_r, low_r]))
+        return [(done[i * N : i * N + N, :N], done[i * N : i * N + N, N:]) for i in range(len(waves))]
 
     def product(a, b):
         return a[0] * b[0] - a[1] * b[1], a[0] * b[1] + a[1] * b[0]
@@ -199,13 +196,9 @@
 
     SPREAD, SPREAD_ADJ, DFT, DFT_INV = 0, 1, 2, 3
 
-    def loop(stage, start, stop):
-        def step(g, carry):
-            for pair in range(GROUP // 2):
-                stage([g * GROUP + 2 * pair, g * GROUP + 2 * pair + 1])
-            return carry
-
-        lax.fori_loop(start // GROUP, stop // GROUP, step, 0)
+    def loop(stage):
+        for start in range(0, SLOTS, GROUP):
+            stage(range(start, start + GROUP))
 
     def ahead(slots):
         illum = (probe_ref[0], probe_ref[1])
@@ -234,19 +227,20 @@
 
     def gather(s):
         def step(block, carry):
-            at = block * 8
-            sums = [jnp.zeros((8, N), F32)] * (2 * LANES)
+            at = block * STRIP
+            sums = [jnp.zeros((STRIP, N), F32)] * (2 * LANES)
             for k in range(SLOTS):
-                from_row = jnp.clip(at - lax.rem(pos_ref[0, k], T) + 8, 0, GROWS - 8)
-                sums = [
-                    total + grad_ref[k, i // LANES, i % LANES, pl.ds(from_row, 8), :]
-                    for i, total in enumerate(sums)
-                ]
+                from_row = jnp.clip(at - lax.rem(pos_ref[0, k], T) + STRIP, 0, GROWS - STRIP)
+                keep = [tall([mask_ref[k, t]] * (STRIP // 8)) for t in range(LANES)]
+                for c in range(2):
+                    part = grad_ref[k, c, pl.ds(from_row, STRIP), :]
+                    for t in range(LANES):
+                        sums[c * LANES + t] = sums[c * LANES + t] + part * keep[t]
             for i, total in enumerate(sums):
-                acc[s][i // LANES, i % LANES, pl.ds(pl.multiple_of(at, 8), 8), :] = total
+                acc[s][i // LANES, i % LANES, pl.ds(pl.multiple_of(at, STRIP), STRIP), :] = total
             return carry
 
-        lax.fori_loop(0, E // 8, step, 0)
+        lax.fori_loop(0, E // STRIP, step, 0)
 
     def mid_start(s):
         rows = [
@@ -321,27 +315,27 @@
             out_ref[s, c, :, N : 2 * N] = jnp.where(low_t, middle, end)
 
     border(0)
-    loop(ahead, 0, SLOTS)
+    loop(ahead)
     border(1)
-    loop(detect, 0, SLOTS)
+    loop(detect)
     gather(1)
     one = mid_start(1)
-    loop(behind, 0, SLOTS // 2)
+    loop(behind)
+    gather(0)
+    zero = mid_start(0)
     one = mid_next(1, one)
-    loop(behind, SLOTS // 2, SLOTS)
-    gather(0)
-    mid_end(0, mid_next(0, mid_start(0)))
-
-    loop(ahead, 0, SLOTS)
+    mid_end(0, mid_next(0, zero))
+
+    loop(ahead)
     mid_end(1, one)
-    loop(detect, 0, SLOTS)
+    loop(detect)
     gather(1)
     one = fin_start(1)
-    loop(behind, 0, SLOTS // 2)
+    loop(behind)
+    gather(0)
+    zero = fin_start(0)
     one = fin_next(1, one)
-    loop(behind, SLOTS // 2, SLOTS)
-    gather(0)
-    zero = fin_next(0, fin_start(0))
+    zero = fin_next(0, zero)
     fin_end(1, one)
     fin_end(0, zero)
 
@@ -368,7 +362,8 @@
                 pltpu.VMEM((2, LANES, E, N), F32),
                 pltpu.VMEM((SLOTS, 2, N, N), F32),
                 pltpu.VMEM((SLOTS, 2, N, N), F32),
-                pltpu.VMEM((SLOTS, 2, LANES, GROWS, N), F32),
+                pltpu.VMEM((SLOTS, 2, GROWS, N), F32),
+                pltpu.VMEM((SLOTS, LANES, 8, N), F32),
                 pltpu.VMEM((2, 2, T, N), F32),
                 pltpu.VMEM((2, 2, T, N), F32),
                 pltpu.VMEM((2, 2, LANES, N, N), F32),

time: 106 us -> 81.6 us (0.77)
  Pallas kernels: 103 us -> 78.5 us
    pallas_call x1, Pallas kernels: 103 us -> 78.5 us  [body(): call(scan_pos.reshape(2, SLOTS), scan_count, object_slices, probe, amplit...]
where the time goes in v2:
time: 81.6 us; the launch traced here: 81.5 us
  Pallas kernels  78.5 us (96%)
  local copies, waits for them, and re-layouts  2.29 us (3%)
    pallas_call x1, Pallas kernels, body(): call(scan_pos.reshape(2, SLOTS), scan_count, object_slices, probe, amplit...  78.5 us
    unnamed x1, local copies, waits for them, and re-layouts  2.29 us

profile of v2, /device:TPU:0, one launch (start us, length us, event | category | flops | bytes accessed | tf_op | source)
XLA Modules:
  0.0 81.5 jit_solution(13253097311667266459)
XLA Ops:
  0.7 78.5 %shard_map.64 = f32[2,2,256,256]{3,2,1,0:T(8,128)} custom-call(s32[2,16]{1,0:T(2,128)} %bitcast.3, s32[1,1]{1,0:T(1,128)S(6)} %copy.8.count_ref, f32[2,2,256,256]{3,2,1,0:T(8,128)} %obj_ref.1, f32[2,128,128]{2,1,0:T(8,128)} %probe_ref.1, f32[16,128,128]{2,1,0:T(8,128)} %bitcast.2, bf16[8,256,256]{2,1,0:T(8,128)(2,1)} %constant.2.clone.tab_ref), custom_call_target="tpu_custom_call" | custom-call | tf_op jit(solution)/shard_map/pallas_call | solution.py:384
  79.2 2.3 %copy.9 = f32[2,2,256,256]{3,2,1,0:T(8,128)} copy(f32[2,2,256,256]{3,2,1,0:T(8,128)} %shard_map.64) | data formatting | bytes 2097152

commit v3 on v2

v3 whole, which is shorter than its diff:
```python
import functools
import math

import jax
import jax.numpy as jnp
import numpy as np
from jax import lax
from jax.experimental import pallas as pl
from jax.experimental.pallas import tpu as pltpu
from jax.sharding import PartitionSpec as P

ITERS = 2
MESH = pl.DeviceIdType.MESH
F32 = jnp.float32
BF16 = jnp.bfloat16

modulus_offset = 0.5
fresnel_scale = 0.9

N = 128
T = 256
E = T + N
HALF = N // 2
LANES = E // N
SLOTS = 16
GROUP = 8
STRIP = 64
SHIFTED = N + 8
GROWS = SHIFTED + 2 * STRIP


def tables():
    positions = np.arange(N)
    frequency = np.where(positions < N // 2, positions, positions - N).astype(np.float64)
    angle = -2.0 * math.pi / N * (np.outer(positions, positions) % N)
    dft = (np.cos(angle) + 1j * np.sin(angle)) / math.sqrt(N)
    phase = math.pi * fresnel_scale * frequency**2 / N
    spread = np.conj(dft) @ (np.exp(1j * phase)[:, None] * dft)
    spread = 0.5 * (spread + spread.T)
    made = []
    for matrix in (spread, dft):
        left = np.block([[matrix.real, -matrix.imag], [matrix.imag, matrix.real]])
        for form in (left, left.T):
            high = form.astype(np.float32).astype(BF16)
            low = (form - high.astype(np.float64)).astype(np.float32).astype(BF16)
            made += [high, low]
    return np.stack(made)


def split(value):
    high = value.astype(BF16)
    return high, (value - high.astype(F32)).astype(BF16)


def dot(a, b):
    return jnp.dot(a, b, preferred_element_type=F32)


def kernel(
    rows_n, cols_n,
    pos_ref, count_ref, obj_hbm, probe_hbm, amps_hbm, tab_hbm,
    out_hbm,
    obj_ref, probe_ref, amps_ref, tab_ref, out_ref,
    ext0, ext1, acc0, acc1, inc_ref, lay_ref, grad0, grad1, mask_ref,
    halo_src, halo_dst, fin_src, fin_dst, up_ref, down_ref,
    send_sem, recv_sem, local_sem,
):
    row, col = lax.axis_index("row"), lax.axis_index("col")
    above, below = lax.rem(row + rows_n - 1, rows_n), lax.rem(row + 1, rows_n)
    before, behind_col = lax.rem(col + cols_n - 1, cols_n), lax.rem(col + 1, cols_n)
    up, down, left, right = (above, col), (below, col), (row, before), (row, behind_col)
    corners = (((above, before), (below, before)), ((above, behind_col), (below, behind_col)))
    has_up, has_down = row > 0, row < rows_n - 1
    has_left, has_right = col > 0, col < cols_n - 1
    ext, acc, grads = (ext0, ext1), (acc0, acc1), (grad0, grad1)
    used = [0]

    barrier = pltpu.get_barrier_semaphore()
    for device in (*corners[0], *corners[1], left, right, up, down):
        pl.semaphore_signal(barrier, inc=1, device_id=device, device_id_type=MESH)

    def load(source, target, index):
        made = pltpu.make_async_copy(source, target, local_sem.at[index])
        made.start()
        return made

    object_in = [load(obj_hbm.at[s], obj_ref.at[s], s) for s in range(2)]
    probe_in = load(probe_hbm, probe_ref, 2)
    tab_in = load(tab_hbm, tab_ref, 3)
    amps_in = load(amps_hbm, amps_ref, 4)

    def copy(source, target, device):
        index = used[0]
        used[0] += 1
        made = pltpu.make_async_remote_copy(
            src_ref=source, dst_ref=target, send_sem=send_sem.at[index],
            recv_sem=recv_sem.at[index], device_id=device, device_id_type=MESH,
        )
        made.start()
        return made

    def wait(copies):
        for made in copies:
            made.wait()

    lane = lax.broadcasted_iota(jnp.int32, (N, N), 1)

    def swap(value):
        return pltpu.roll(value, HALF, 1)

    def lows(value):
        return lax.broadcasted_iota(jnp.int32, value.shape, 1) < HALF

    def pick(in_low, in_high):
        return jnp.where(lows(in_low), in_low, in_high)

    def place(k):
        at_row, at_col = pos_ref[0, k], pos_ref[1, k]
        return (at_row >> 3) & (T // 8 - 1), at_row & 7, (at_col >> 7) & 1, at_col & (N - 1)

    def prepare(k, carry):
        _, _, at_lane, shift = place(k)
        live = (k < count_ref[0, 0]).astype(F32)
        upper = (lax.broadcasted_iota(jnp.int32, (8, N), 1) >= shift).astype(F32)
        mask_ref[k, 0] = upper * live
        mask_ref[k, 1] = (1.0 - upper) * live
        mask_ref[k, 2] = jnp.zeros((8, N), F32) + (1 - at_lane).astype(F32)
        for c in range(2):
            for half in range(2):
                for grad in grads:
                    grad[k, c, half, 0:STRIP, :] = jnp.zeros((STRIP, N), F32)
                    grad[k, c, half, GROWS - STRIP : GROWS, :] = jnp.zeros((STRIP, N), F32)
        return carry

    own, head, tail = slice(HALF, HALF + T), slice(0, HALF), slice(HALF + T, E)

    def edges(source, target, s):
        made = []
        begin = source.shape[2] - T
        first, last, whole = slice(0, HALF), slice(source.shape[2] - HALF, source.shape[2]), slice(begin // 2, begin // 2 + T)
        for side in range(2):
            made.append(copy(source.at[s, side, first], target.at[s, 1 - side, tail], corners[side][0]))
            made.append(copy(source.at[s, side, last], target.at[s, 1 - side, head], corners[side][1]))
        for side, device in enumerate((left, right)):
            made.append(copy(source.at[s, side, whole], target.at[s, 1 - side, own], device))
        return made

    def halo_pack(s):
        halo_src[s, 0] = pick(swap(ext[s][1, 0, own, :]), ext[s][0, 0, own, :])
        halo_src[s, 1] = pick(ext[s][0, 2, own, :], swap(ext[s][1, 2, own, :]))

    def halo_start(s):
        return edges(halo_src, halo_dst, s) + [
            copy(ext[s].at[:, :, HALF : 2 * HALF, :], ext[s].at[:, :, tail, :], up),
            copy(ext[s].at[:, :, T : T + HALF, :], ext[s].at[:, :, head, :], down),
        ]

    def halo_end(s, copies):
        wait(copies)
        for part, inside in ((head, has_up), (own, None), (tail, has_down)):
            for t in range(LANES):
                if t == 1 and inside is None:
                    continue
                for c in range(2):
                    value = ext[s][c, t, part, :]
                    if t != 1:
                        strip = jnp.where((has_left, None, has_right)[t], halo_dst[s, t // 2, part, :], 0.0)
                        strip = strip if c == 0 else swap(strip)
                        value = pick(strip, value) if t == 0 else pick(value, strip)
                    ext[s][c, t, part, :] = value if inside is None else jnp.where(inside, value, 0.0)

    def grad_start(s):
        fin_src[s, 0] = pick(acc[s][0, 0], swap(acc[s][1, 0]))
        fin_src[s, 1] = pick(swap(acc[s][1, 2]), acc[s][0, 2])
        return edges(fin_src, fin_dst, s) + [
            copy(acc[s].at[:, :, head, :], down_ref.at[s], up),
            copy(acc[s].at[:, :, tail, :], up_ref.at[s], down),
        ]

    def grad_end(s, copies, last):
        wait(copies)
        for p in range(T // HALF):
            part = slice(HALF * (p + 1), HALF * (p + 2))
            strips = []
            for side, there in enumerate((has_left, has_right)):
                strip = fin_dst[s, side, part, :]
                if p == 0:
                    strip = strip + jnp.where(has_up, fin_dst[s, side, head, :], 0.0)
                if p == T // HALF - 1:
                    strip = strip + jnp.where(has_down, fin_dst[s, side, tail, :], 0.0)
                strips.append(jnp.where(there, strip, 0.0))
            for c in range(2):
                made = []
                for t in range(LANES):
                    value = ext[s][c, t, part, :] - acc[s][c, t, part, :]
                    if t != 1:
                        value = value - (strips[t // 2] if c == 0 else swap(strips[t // 2]))
                    if p == 0:
                        value = value - jnp.where(has_up, up_ref[s, c, t], 0.0)
                    if p == T // HALF - 1:
                        value = value - jnp.where(has_down, down_ref[s, c, t], 0.0)
                    made.append(value)
                if last:
                    made = [swap(value) for value in made]
                    out_ref[s, c, HALF * p : HALF * (p + 1), 0:N] = pick(made[0], made[1])
                    out_ref[s, c, HALF * p : HALF * (p + 1), N : 2 * N] = pick(made[1], made[2])
                else:
                    for t in range(LANES):
                        ext[s][c, t, part, :] = made[t]

    def patch(s, k):
        eighth, over, at_lane, shift = place(k)
        rows = pl.ds(eighth * 8, SHIFTED)
        parts = []
        for c in range(2):
            here, after = ext[s][c, at_lane, rows, :], ext[s][c, at_lane + 1, rows, :]
            both = jnp.where(lax.broadcasted_iota(jnp.int32, (SHIFTED, N), 1) >= shift, here, after)
            both = pltpu.roll(both, 8 - over, 0)[SHIFTED - N :]
            parts.append(pltpu.roll(both, (N - shift) & (N - 1), 1))
        return parts

    def put(s, k, parts):
        _, over, _, shift = place(k)
        for c in range(2):
            moved = tall([pltpu.roll(parts[c], shift, 1), jnp.zeros((SHIFTED - N, N), F32)])
            moved = pltpu.roll(moved, over, 0)
            for half in range(2):
                grads[s][k, c, half, STRIP : STRIP + SHIFTED, :] = moved * tall([mask_ref[k, half]] * (SHIFTED // 8))

    def tall(parts):
        return jnp.concatenate(parts, axis=0)

    def wide(parts):
        return jnp.concatenate(parts, axis=1)

    def apply(which, waves):
        high_l, low_l = tab_ref[2 * which], tab_ref[2 * which + 1]
        other = which ^ 1
        high_r, low_r = tab_ref[2 * other], tab_ref[2 * other + 1]
        high, low_part = split(tall([wide([wave[c] for wave in waves]) for c in range(2)]))
        mid = dot(wide([high_l, high_l, low_l]), tall([high, low_part, high]))
        high, low_part = split(
            tall([wide([mid[:N, i * N : i * N + N], mid[N:, i * N : i * N + N]]) for i in range(len(waves))])
        )
        done = dot(wide([high, low_part, high]), tall([high_r, high_r, low_r]))
        return [(done[i * N : i * N + N, :N], done[i * N : i * N + N, N:]) for i in range(len(waves))]

    def product(a, b):
        return a[0] * b[0] - a[1] * b[1], a[0] * b[1] + a[1] * b[0]

    def product_conj(a, b):
        return a[0] * b[0] + a[1] * b[1], a[0] * b[1] - a[1] * b[0]

    SPREAD, SPREAD_ADJ, DFT, DFT_INV = 0, 1, 2, 3

    def loop(stage):
        for start in range(0, SLOTS, GROUP):
            stage(range(start, start + GROUP))

    def ahead(slots):
        illum = (probe_ref[0], probe_ref[1])
        waves = apply(SPREAD, [product(illum, patch(0, k)) for k in slots])
        for k, wave in zip(slots, waves):
            inc_ref[k, 0], inc_ref[k, 1] = wave

    def detect(slots):
        exits = []
        for k in slots:
            layer = patch(1, k)
            lay_ref[k, 0], lay_ref[k, 1] = layer
            exits.append(product((inc_ref[k, 0], inc_ref[k, 1]), layer))
        residuals = []
        for k, (re, im) in zip(slots, apply(DFT, exits)):
            factor = 1.0 - amps_ref[k] / jnp.sqrt(re * re + im * im + modulus_offset)
            residuals.append((re * factor, im * factor))
        for k, back in zip(slots, apply(DFT_INV, residuals)):
            put(1, k, product_conj((inc_ref[k, 0], inc_ref[k, 1]), back))
            lay_ref[k, 0], lay_ref[k, 1] = product_conj((lay_ref[k, 0], lay_ref[k, 1]), back)

    def behind(slots):
        illum = (probe_ref[0], probe_ref[1])
        for k, back in zip(slots, apply(SPREAD_ADJ, [(lay_ref[k, 0], lay_ref[k, 1]) for k in slots])):
            put(0, k, product_conj(illum, back))

    def strips_of(s, k, half, at):
        from_row = jnp.clip(at - place(k)[0] + STRIP // 8, 0, (GROWS - STRIP) // 8) * 8
        return [grads[s][k, c, half, pl.ds(from_row, STRIP), :] for c in range(2)]

    def gather_sides(s):
        def step(block, carry):
            at = block * STRIP
            both = [jnp.zeros((STRIP, N), F32)] * 2
            first = [jnp.zeros((STRIP, N), F32)] * 2
            for k in range(SLOTS):
                keep = tall([mask_ref[k, 2]] * (STRIP // 8))
                for c, part in enumerate(strips_of(s, k, place(k)[2], block * (STRIP // 8))):
                    both[c] = both[c] + part
                    first[c] = first[c] + part * keep
            for c in range(2):
                acc[s][c, 0, pl.ds(pl.multiple_of(at, STRIP), STRIP), :] = first[c]
                acc[s][c, 2, pl.ds(pl.multiple_of(at, STRIP), STRIP), :] = both[c] - first[c]
            return carry

        lax.fori_loop(0, E // STRIP, step, 0)

    def gather_middle(s, number, strip_at):
        def step(block, carry):
            at = strip_at(block) * STRIP
            total = [jnp.zeros((STRIP, N), F32)] * 2
            for k in range(SLOTS):
                for c, part in enumerate(strips_of(s, k, 1 - place(k)[2], strip_at(block) * (STRIP // 8))):
                    total[c] = total[c] + part
            for c in range(2):
                acc[s][c, 1, pl.ds(pl.multiple_of(at, STRIP), STRIP), :] = total[c]
            return carry

        lax.fori_loop(0, number, step, 0)

    def exchange(s):
        rim = HALF // STRIP
        gather_middle(s, 2 * rim, lambda i: i + (i // rim) * (T // STRIP))
        gather_sides(s)
        made = grad_start(s)
        gather_middle(s, T // STRIP, lambda i: i + rim)
        return made

    for s in range(2):
        object_in[s].wait()
        for c in range(2):
            first, last = swap(obj_ref[s, c, :, 0:N]), swap(obj_ref[s, c, :, N : 2 * N])
            ext[s][c, 0, own, :] = first
            ext[s][c, 1, own, :] = pick(first, last)
            ext[s][c, 2, own, :] = last
        halo_pack(s)
    lax.fori_loop(0, SLOTS, prepare, 0)
    probe_in.wait()
    tab_in.wait()
    amps_in.wait()
    pl.semaphore_wait(barrier, 8)
    halos = [halo_start(s) for s in range(2)]

    for iteration in range(ITERS):
        last = iteration == ITERS - 1
        halo_end(0, halos[0])
        loop(ahead)
        halo_end(1, halos[1])
        loop(detect)
        if last:
            one = exchange(1)
            loop(behind)
            zero = exchange(0)
        else:
            loop(behind)
            zero = exchange(0)
            one = exchange(1)
        stores = []
        for s, copies in ((1, one), (0, zero)) if last else ((0, zero), (1, one)):
            grad_end(s, copies, last)
            if last:
                stores.append(load(out_ref.at[s], out_hbm.at[s], 5 + s))
            else:
                halo_pack(s)
                halos[s] = halo_start(s)
    for made in stores:
        made.wait()


COPIES = 64


def solution(mesh):
    rows_n, cols_n = mesh.shape["row"], mesh.shape["col"]
    hbm = pl.BlockSpec(memory_space=pl.ANY)
    smem = pl.BlockSpec(memory_space=pltpu.SMEM)

    def body(object_slices, probe, amplitudes, scan_pos, scan_count):
        tab = jnp.asarray(tables())
        call = pl.pallas_call(
            functools.partial(kernel, rows_n, cols_n),
            out_shape=jax.ShapeDtypeStruct(object_slices.shape, F32),
            in_specs=[smem, smem, hbm, hbm, hbm, hbm],
            out_specs=hbm,
            scratch_shapes=[
                pltpu.VMEM((2, 2, T, T), F32),
                pltpu.VMEM((2, N, N), F32),
                pltpu.VMEM((SLOTS, N, N), F32),
                pltpu.VMEM((8, 2 * N, 2 * N), BF16),
                pltpu.VMEM((2, 2, T, T), F32),
                pltpu.VMEM((2, LANES, E, N), F32),
                pltpu.VMEM((2, LANES, E, N), F32),
                pltpu.VMEM((2, LANES, E, N), F32),
                pltpu.VMEM((2, LANES, E, N), F32),
                pltpu.VMEM((SLOTS, 2, N, N), F32),
                pltpu.VMEM((SLOTS, 2, N, N), F32),
                pltpu.VMEM((SLOTS, 2, 2, GROWS, N), F32),
                pltpu.VMEM((SLOTS, 2, 2, GROWS, N), F32),
                pltpu.VMEM((SLOTS, 3, 8, N), F32),
                pltpu.VMEM((2, 2, T, N), F32),
                pltpu.VMEM((2, 2, E, N), F32),
                pltpu.VMEM((2, 2, E, N), F32),
                pltpu.VMEM((2, 2, E, N), F32),
                pltpu.VMEM((2, 2, LANES, HALF, N), F32),
                pltpu.VMEM((2, 2, LANES, HALF, N), F32),
                pltpu.SemaphoreType.DMA((COPIES,)),
                pltpu.SemaphoreType.DMA((COPIES,)),
                pltpu.SemaphoreType.DMA((7,)),
            ],
            compiler_params=pltpu.CompilerParams(
                collective_id=0, has_side_effects=True, vmem_limit_bytes=56 * 2**20
            ),
        )
        return call(
            scan_pos.reshape(2, SLOTS), scan_count, object_slices, probe,
            amplitudes.reshape(SLOTS, N, N), tab,
        )

    in_specs = (
        P(None, None, "row", "col"),
        P(),
        P("row", "col", None, None, None),
        P(None, "row", "col", None),
        P("row", "col"),
    )
    out_specs = P(None, None, "row", "col")
    return jax.shard_map(body, mesh=mesh, in_specs=in_specs, out_specs=out_specs, check_vma=False)
```

time: 81.6 us -> 76.9 us (0.942)
  Pallas kernels: 78.5 us -> 73.8 us
    pallas_call x1, Pallas kernels: 78.5 us -> 73.8 us  [body(): call(scan_pos.reshape(2, SLOTS), scan_count, object_slices, probe, amplit...]
where the time goes in v3:
time: 76.9 us; the launch traced here: 76.7 us
  Pallas kernels  73.8 us (96%)
  local copies, waits for them, and re-layouts  2.29 us (3%)
    pallas_call x1, Pallas kernels, body(): call(scan_pos.reshape(2, SLOTS), scan_count, object_slices, probe, amplit...  73.8 us
    unnamed x1, local copies, waits for them, and re-layouts  2.29 us

profile of v3, /device:TPU:0, one launch (start us, length us, event | category | flops | bytes accessed | tf_op | source)
XLA Modules:
  0.0 76.7 jit_solution(10696798677673985247)
XLA Ops:
  0.7 73.8 %shard_map.64 = f32[2,2,256,256]{3,2,1,0:T(8,128)} custom-call(s32[2,16]{1,0:T(2,128)} %bitcast.3, s32[1,1]{1,0:T(1,128)S(6)} %copy.8.count_ref, f32[2,2,256,256]{3,2,1,0:T(8,128)} %obj_hbm.1, f32[2,128,128]{2,1,0:T(8,128)} %probe_hbm.1, f32[16,128,128]{2,1,0:T(8,128)} %bitcast.2, bf16[8,256,256]{2,1,0:T(8,128)(2,1)} %constant.2.clone.tab_hbm), custom_call_target="tpu_custom_call" | custom-call | tf_op jit(solution)/shard_map/pallas_call | solution.py:412
  74.4 2.3 %copy.9 = f32[2,2,256,256]{3,2,1,0:T(8,128)} copy(f32[2,2,256,256]{3,2,1,0:T(8,128)} %shard_map.64) | data formatting | bytes 2097152

commit v4 on v3

--- a/solution.py
+++ b/solution.py
@@ -23,7 +23,7 @@
 HALF = N // 2
 LANES = E // N
 SLOTS = 16
-GROUP = 8
+GROUP = 4
 STRIP = 64
 SHIFTED = N + 8
 GROWS = SHIFTED + 2 * STRIP
@@ -172,7 +172,10 @@
     def grad_start(s):
         fin_src[s, 0] = pick(acc[s][0, 0], swap(acc[s][1, 0]))
         fin_src[s, 1] = pick(swap(acc[s][1, 2]), acc[s][0, 2])
-        return edges(fin_src, fin_dst, s) + [
+        made = edges(fin_src, fin_dst, s)
+        rim = HALF // STRIP
+        gather_middle(s, 2 * rim, lambda i: i + (i // rim) * (T // STRIP))
+        return made + [
             copy(acc[s].at[:, :, head, :], down_ref.at[s], up),
             copy(acc[s].at[:, :, tail, :], up_ref.at[s], down),
         ]
@@ -271,7 +274,7 @@
             exits.append(product((inc_ref[k, 0], inc_ref[k, 1]), layer))
         residuals = []
         for k, (re, im) in zip(slots, apply(DFT, exits)):
-            factor = 1.0 - amps_ref[k] / jnp.sqrt(re * re + im * im + modulus_offset)
+            factor = 1.0 - amps_ref[k] * lax.rsqrt(re * re + im * im + modulus_offset)
             residuals.append((re * factor, im * factor))
         for k, back in zip(slots, apply(DFT_INV, residuals)):
             put(1, k, product_conj((inc_ref[k, 0], inc_ref[k, 1]), back))
@@ -317,11 +320,9 @@
         lax.fori_loop(0, number, step, 0)
 
     def exchange(s):
-        rim = HALF // STRIP
-        gather_middle(s, 2 * rim, lambda i: i + (i // rim) * (T // STRIP))
         gather_sides(s)
         made = grad_start(s)
-        gather_middle(s, T // STRIP, lambda i: i + rim)
+        gather_middle(s, T // STRIP, lambda i: i + HALF // STRIP)
         return made
 
     for s in range(2):

time: 76.9 us -> 75.6 us (0.983)
  Pallas kernels: 73.8 us -> 72.5 us
    pallas_call x1, Pallas kernels: 73.8 us -> 72.5 us  [body(): call(scan_pos.reshape(2, SLOTS), scan_count, object_slices, probe, amplit...]
where the time goes in v4:
time: 75.6 us; the launch traced here: 75.5 us
  Pallas kernels  72.5 us (96%)
  local copies, waits for them, and re-layouts  2.29 us (3%)
    pallas_call x1, Pallas kernels, body(): call(scan_pos.reshape(2, SLOTS), scan_count, object_slices, probe, amplit...  72.5 us
    unnamed x1, local copies, waits for them, and re-layouts  2.29 us

profile of v4, /device:TPU:0, one launch (start us, length us, event | category | flops | bytes accessed | tf_op | source)
XLA Modules:
  0.0 75.5 jit_solution(11761549543043284813)
XLA Ops:
  0.7 72.5 %shard_map.64 = f32[2,2,256,256]{3,2,1,0:T(8,128)} custom-call(s32[2,16]{1,0:T(2,128)} %bitcast.3, s32[1,1]{1,0:T(1,128)S(6)} %copy.8.count_ref, f32[2,2,256,256]{3,2,1,0:T(8,128)} %obj_hbm.1, f32[2,128,128]{2,1,0:T(8,128)} %probe_hbm.1, f32[16,128,128]{2,1,0:T(8,128)} %bitcast.2, bf16[8,256,256]{2,1,0:T(8,128)(2,1)} %constant.2.clone.tab_hbm), custom_call_target="tpu_custom_call" | custom-call | tf_op jit(solution)/shard_map/pallas_call | solution.py:413
  73.2 2.3 %copy.9 = f32[2,2,256,256]{3,2,1,0:T(8,128)} copy(f32[2,2,256,256]{3,2,1,0:T(8,128)} %shard_map.64) | data formatting | bytes 2097152
